TPU v7x, 32 devices: a whole 2x2x4 slice. The times are simulated.
32 devices in a mesh: gx: 4 (over x, core), gy: 8 (over z, y).
Axes of the slice: x: 2, y: 2, z: 4, core: 2. Of those that a mesh axis runs over, the one named last changes fastest.
Arguments:
- state: float32 [10, 32, 64, 128], P(None, 'gx', 'gy'), may hold values from 0.01 to 3, as said below
- source_in: float32 [10, 32, 64, 128], P(None, 'gx', 'gy'), may hold values from -3 to 3
- counts: int32 [32, 64], P('gx', 'gy'), may hold values from 1 to 8, as said below
- diffusivity: float32 [10], replicated, may hold values from 0.3 to 1
- log_rate: float32 [21], replicated, may hold values from 0.3 to 1
- activation: float32 [21], replicated, may hold values from 0.4 to 0.8
- heat_release: float32 [21], replicated, may hold values from -1 to 2
Outputs:
- next_state: float32 [10, 32, 64, 128], P(None, 'gx', 'gy')
- late_source: float32 [10, 32, 64, 128], P(None, 'gx', 'gy')
Inputs may be any that keep to these rules, and one draw needn't show every extreme that they name: Boxes of 8 x 8 blocks are either flame boxes, about an eighth of them, where every count is 5 or more and one is 8, or others, where counts are 1 or 2. `state`: rows 0 to 8 lie in [0.01, 1]; the last row lies in [1, 3].
All inputs are finite; a program needn't handle non-finite values.
Results may differ from a plain program's by a relative error of at most 0.0003.
Values sent between devices are 32-bit elements; how exact they have to be, the bound alone decides.
A program may use at most 64 MiB of HBM per device.

v0:
```python
import jax
import jax.numpy as jnp
import numpy as np
from jax import lax
from jax.experimental import pallas as pl
from jax.experimental.pallas import tpu as pltpu
from jax.sharding import PartitionSpec as P

time_step = 0.15
log2_e = 1.4426950408889634
most_steps = 8
late_steps = 2
together = 2
reaction_table = (
    (3, 1, (4, 5)),
    (4, 0, (3, 5)),
    (5, 0, (3, 2)),
    (5, 5, (4, 2)),
    (3, 3, (0,)),
    (3, 5, (2,)),
    (4, 4, (1,)),
    (3, 4, (5,)),
    (3, 1, (6,)),
    (6, 3, (0, 1)),
    (6, 3, (5, 5)),
    (6, 4, (1, 5)),
    (6, 5, (2, 1)),
    (6, 6, (7, 1)),
    (7, 9, (5, 5)),
    (7, 3, (2, 5)),
    (7, 3, (6, 0)),
    (7, 4, (5, 6)),
    (7, 5, (6, 2)),
    (0, 9, (3, 3)),
    (2, 9, (3, 5)),
)
free_rows = (0, 1, 2, 4, 6, 7)
spanning = (7, 11, 14, 17, 19, 20)


def spanning_tables():
    change = np.zeros((9, 21))
    for reaction, (one, two, products) in enumerate(reaction_table):
        change[one, reaction] -= 1.0
        if two < 9:
            change[two, reaction] -= 1.0
        for product in products:
            change[product, reaction] += 1.0
    kept = change[list(free_rows)]
    inverse = np.round(np.linalg.inv(kept[:, list(spanning)]), 6)
    return inverse, np.round(inverse @ kept, 6)


def weighted(terms):
    total = None
    for weight, value in terms:
        if weight == 0:
            continue
        term = value if weight == 1 else value * float(weight)
        total = term if total is None else total + term
    return total


def heat_scalars(heat):
    inverse, spans = spanning_tables()
    base = [heat[r] for r in spanning]
    on_rows = [weighted([(inverse[i, j], base[i]) for i in range(6)]) for j in range(6)]
    on_reactions = {}
    for r in range(21):
        if r not in spanning:
            on_reactions[r] = weighted([(1.0, heat[r])] + [(-spans[i, r], base[i]) for i in range(6)])
    return on_rows, on_reactions


def prepare(temperature, stride, log_rate, activation):
    inverse_t = 1.0 / temperature
    return [jnp.exp2(log_rate[r] * log2_e - (activation[r] * log2_e) * inverse_t) * stride for r in range(21)]


def atoms(u):
    h2, o2, h2o, h, o, oh, ho2, h2o2 = u
    oxygen = 2.0 * (o2 + ho2 + h2o2) + h2o + o + oh
    surplus = 2.0 * (h2 - o2) + h2o + h - ho2 - o
    return oxygen, surplus


def substep(u, kept, k, active):
    h2, o2, h2o, h, o, oh, ho2, h2o2 = u
    oxygen, surplus = kept
    a, b, c, d, e, f, g = (h2, h2o, h, o, oh, ho2, h2o2)
    if active is not None:
        a, b, c, d, e, f, g = [jnp.where(active, v, 0.0) for v in (a, b, c, d, e, f, g)]
    p = {0: c * o2, 1: d * a, 2: e * a, 3: e * e, 4: c * c, 5: c * e, 6: d * d, 9: f * c, 12: f * e, 13: f * f,
         15: g * c, 18: g * e}
    w = {r: k[r] * v for r, v in p.items()}
    w[8] = k[8] * p[0]
    w[10] = k[10] * p[9]
    w[16] = k[16] * p[15]
    w[7] = k[7] * (c * d)
    w[11] = k[11] * (f * d)
    w[17] = k[17] * (g * d)
    w[14] = k[14] * g
    w[19] = k[19] * a
    w[20] = k[20] * b
    s1 = w[16] + w[17] + w[18]
    s2 = (w[9] + w[13]) + (w[11] + w[12])
    h2 = h2 + (((w[4] + w[9]) + (w[16] - w[1])) - (w[2] + w[19]))
    o2 = o2 + ((s2 + w[6]) - (w[0] + w[8]))
    h2o = h2o + (((w[2] + w[3]) + (w[5] + w[12])) + ((w[15] + w[18]) - w[20]))
    o = o + (((w[0] + w[3]) - (w[1] + w[7])) - ((w[6] + w[6]) + (w[11] + w[17])))
    ho2 = ho2 + (((s1 + w[8]) - s2) - (w[10] + w[13]))
    h2o2 = h2o2 + ((w[13] - s1) - (w[14] + w[15]))
    oh = ((oxygen - h2o) - o) - 2.0 * ((o2 + ho2) + h2o2)
    h = ((surplus - h2o) + (ho2 + o)) - 2.0 * (h2 - o2)
    return (h2, o2, h2o, h, o, oh, ho2, h2o2), p


def warmth(change, sums, k, heat):
    on_rows, on_reactions = heat_scalars(heat)
    rate = {r: on_reactions[r] * k[r] for r in on_reactions}
    rate[0] = rate[0] + rate.pop(8)
    rate[9] = rate[9] + rate.pop(10)
    rate[15] = rate[15] + rate.pop(16)
    terms = [rate[r] * total for r, total in sums.items()]
    terms += [weight * change[row] for weight, row in zip(on_rows, free_rows)]
    while len(terms) > 1:
        terms = [sum(terms[i + 1:i + 2], terms[i]) for i in range(0, len(terms), 2)]
    return terms[0]


def chemistry(u, counts, stride, log_rate, activation, heat, done, upto):
    k = prepare(u[9], stride, log_rate, activation)
    before = tuple(u[:8])
    kept = atoms(before)
    now, sums = before, None
    for turn in range(done, upto):
        now, p = substep(now, kept, k, None if turn == 0 else counts > float(turn))
        sums = p if sums is None else {r: sums[r] + p[r] for r in sums}
    change = [after - start for after, start in zip(now, before)]
    return change + [jnp.zeros_like(u[9]), warmth(change, sums, k, heat)]


def block_numbers(counts, i, row_index, ny):
    number = jnp.zeros(row_index.shape, jnp.int32)
    for j in range(ny):
        number = jnp.where(row_index == j, counts[i, j], number)
    return number.astype(jnp.float32)


def first_kernel(
    state, source, counts_in, diffusivity_in, log_rate_in, activation_in, heat_in,
    first_out, next_out,
    st, src, first, nxt, counts, diffusivity, log_rate, activation, heat, numbers,
    own_y, fx, fy, hx1, hy1, corners, hx2, hy2,
    load_sem, store_sem, send_sem, recv_sem,
):
    rows, nx, ny, nz = st.shape
    x, size_x = lax.axis_index("gx"), lax.axis_size("gx")
    y, size_y = lax.axis_index("gy"), lax.axis_size("gy")
    x_up, x_down = lax.rem(x + 1, size_x), lax.rem(x + size_x - 1, size_x)
    y_up, y_down = lax.rem(y + 1, size_y), lax.rem(y + size_y - 1, size_y)
    sides = ((x_up, y), (x_down, y), (x, y_up), (x, y_down))
    diagonals = ((x_up, y_up), (x_up, y_down), (x_down, y_up), (x_down, y_down))
    barrier = pltpu.get_barrier_semaphore()
    for device in diagonals + sides:
        pl.semaphore_signal(barrier, inc=1, device_id=device, device_id_type=pl.DeviceIdType.MESH)
    pairs = (
        (state, st), (source, src), (diffusivity_in, diffusivity),
        (counts_in, counts), (log_rate_in, log_rate), (activation_in, activation), (heat_in, heat),
        (state.at[:, :, 0], own_y.at[0]), (state.at[:, :, ny - 1], own_y.at[1]),
    )
    loads = [pltpu.make_async_copy(one, two, load_sem.at[n]) for n, (one, two) in enumerate(pairs)]
    for load in loads:
        load.start()

    def send(pieces, devices, base):
        copies = []
        for place, (piece, device) in enumerate(zip(pieces, devices)):
            copies.append(pltpu.make_async_remote_copy(
                src_ref=piece[0], dst_ref=piece[1],
                send_sem=send_sem.at[base + place], recv_sem=recv_sem.at[base + place],
                device_id=device, device_id_type=pl.DeviceIdType.MESH,
            ))
        for copy in copies[::-1]:
            copy.start()
        return copies

    pl.semaphore_wait(barrier, 8)
    state_copies = send((
        (state.at[:, nx - 1], hx1.at[0]),
        (state.at[:, 0], hx1.at[1]),
        (state.at[:, :, ny - 1], hy1.at[0]),
        (state.at[:, :, 0], hy1.at[1]),
    ), sides, 0)
    corner_copies = send((
        (state.at[:, nx - 1, ny - 1], corners.at[0]),
        (state.at[:, nx - 1, 0], corners.at[1]),
        (state.at[:, 0, ny - 1], corners.at[2]),
        (state.at[:, 0, 0], corners.at[3]),
    ), diagonals, 4)

    row_index = lax.broadcasted_iota(jnp.int32, (ny, nz), 0)
    at_low, at_high = row_index == 0, row_index == ny - 1

    def inner_laplace(field, k, i):
        here = field[k, i]
        low = jnp.where(at_low, 0.0, pltpu.roll(here, 1, 0))
        high = jnp.where(at_high, 0.0, pltpu.roll(here, ny - 1, 0))
        beside = (low + high) + (pltpu.roll(here, 1, 1) + pltpu.roll(here, nz - 1, 1))
        if i > 0:
            beside = beside + field[k, i - 1]
        if i < nx - 1:
            beside = beside + field[k, i + 1]
        return beside - 6.0 * here

    def outer_laplace(halo_x, halo_y, k, i):
        low = jnp.where(at_low, halo_y[0, k, pl.ds(i, 1), :], 0.0)
        rest = jnp.where(at_high, halo_y[1, k, pl.ds(i, 1), :], low)
        if i == 0:
            rest = rest + halo_x[0, k]
        if i == nx - 1:
            rest = rest + halo_x[1, k]
        return rest

    def first_inner(k, carry):
        weight = time_step * diffusivity[k]
        for i in range(nx):
            value = (st[k, i] + time_step * src[k, i]) + weight * inner_laplace(st, k, i)
            first[k, i] = value
            fy[0, k, pl.ds(i, 1), :] = value[ny - 1:]
            fy[1, k, pl.ds(i, 1), :] = value[:1]
            if i == nx - 1:
                fx[0, k] = value
            if i == 0:
                fx[1, k] = value
        return carry

    for load in loads[:3]:
        load.wait()
    lax.fori_loop(0, rows, first_inner, 0)
    first_copies = send((
        (fx.at[0], hx2.at[0]), (fx.at[1], hx2.at[1]), (fy.at[0], hy2.at[0]), (fy.at[1], hy2.at[1]),
    ), sides, 8)

    for load in loads[3:]:
        load.wait()
    for i in range(nx):
        numbers[i] = block_numbers(counts, i, row_index, ny)

    def early_group(i, carry):
        part = pl.ds(i * together, together)
        u = [st[s, part] for s in range(rows)]
        number = numbers[part]
        change = chemistry(u, number, time_step / number, log_rate, activation, heat, 0, most_steps)
        for s in range(rows):
            nxt[s, part] = 0.5 * (u[s] + change[s])
        return carry

    lax.fori_loop(0, nx // together, early_group, 0)

    def first_outer(k, carry):
        weight = time_step * diffusivity[k]
        for i in range(nx):
            first[k, i] = first[k, i] + weight * outer_laplace(hx1, hy1, k, i)
        return carry

    for copy in state_copies:
        copy.wait()
    lax.fori_loop(0, rows, first_outer, 0)
    first_store = pltpu.make_async_copy(first, first_out, store_sem.at[0])
    first_store.start()

    def next_inner(k, carry):
        weight = (0.5 * time_step) * diffusivity[k]
        for i in range(nx):
            nxt[k, i] = (nxt[k, i] + 0.5 * first[k, i]) + weight * inner_laplace(first, k, i)
        return carry

    lax.fori_loop(0, rows, next_inner, 0)
    for copy in corner_copies + first_copies:
        copy.wait()

    side_index = lax.broadcasted_iota(jnp.int32, (nx, nz), 0)

    def next_outer(k, carry):
        weight = time_step * diffusivity[k]
        corner = [corners[n, pl.ds(k, 1), :] for n in range(4)]
        for n, plane in ((0, st[k, 0]), (1, st[k, nx - 1])):
            low = jnp.where(at_low, corner[2 * n], 0.0)
            rest = jnp.where(at_high, corner[2 * n + 1], low)
            hx2[n, k] = hx2[n, k] + weight * (plane + rest)
        for n in range(2):
            low = jnp.where(side_index == 0, corner[n], 0.0)
            rest = jnp.where(side_index == nx - 1, corner[2 + n], low)
            hy2[n, k] = hy2[n, k] + weight * (own_y[n, k] + rest)
        for i in range(nx):
            nxt[k, i] = nxt[k, i] + (0.5 * weight) * outer_laplace(hx2, hy2, k, i)
        return carry

    lax.fori_loop(0, rows, next_outer, 0)
    next_store = pltpu.make_async_copy(nxt, next_out, store_sem.at[1])
    next_store.start()
    first_store.wait()
    next_store.wait()


def second_kernel(
    first_in, next_in, counts_in, log_rate_in, activation_in, heat_in,
    next_out, late_out,
    first, nxt, late, counts, log_rate, activation, heat, small_sem, load_sem, next_sem, late_sem,
):
    rows, nx, ny, nz = first.shape
    groups = nx // together
    pairs = ((counts_in, counts), (log_rate_in, log_rate), (activation_in, activation), (heat_in, heat))
    small = [pltpu.make_async_copy(one, two, small_sem.at[n]) for n, (one, two) in enumerate(pairs)]

    def span(i):
        return pl.ds(i * together, together)

    def first_load(i):
        return pltpu.make_async_copy(first_in.at[:, span(i)], first.at[:, span(i)], load_sem.at[i])

    def late_store(i):
        return pltpu.make_async_copy(late.at[:, span(i)], late_out.at[:, span(i)], late_sem.at[i])

    next_load = pltpu.make_async_copy(next_in, nxt, next_sem.at[0])
    next_store = pltpu.make_async_copy(nxt, next_out, next_sem.at[1])
    for copy in small:
        copy.start()
    for i in range(groups):
        first_load(i).start()
    next_load.start()
    for copy in small:
        copy.wait()
    row_index = lax.broadcasted_iota(jnp.int32, (ny, nz), 0)

    def group(i, carry):
        last = counts[i * together, 0]
        for n in range(together):
            for j in range(ny):
                last = jnp.maximum(last, counts[i * together + n, j])
        number = jnp.stack([block_numbers(counts, i * together + n, row_index, ny) for n in range(together)])
        first_load(i).wait()

        def run(upto):
            u = [first[s, span(i)] for s in range(rows)]
            change = chemistry(u, number, time_step / number, log_rate, activation, heat, 0, upto)
            for s in range(rows):
                late[s, span(i)] = change[s] * (1.0 / time_step)

        @pl.when(last <= late_steps)
        def _():
            run(late_steps)

        @pl.when(last > late_steps)
        def _():
            run(most_steps)

        late_store(i).start()

        @pl.when(i == 0)
        def _():
            next_load.wait()
            next_store.start()

        return carry

    lax.fori_loop(0, groups, group, 0)
    next_store.wait()
    for i in range(groups):
        late_store(i).wait()


def local(state, source_in, counts, diffusivity, log_rate, activation, heat_release):
    rows, nx, ny, nz = state.shape
    whole = jax.ShapeDtypeStruct(state.shape, jnp.float32)
    field = pltpu.VMEM(state.shape, jnp.float32)
    outside = pl.BlockSpec(memory_space=pl.ANY)
    scalars = [pltpu.SMEM(a.shape, a.dtype) for a in (counts, log_rate, activation, heat_release)]
    halo_x = pltpu.VMEM((2, rows, ny, nz), jnp.float32)
    halo_y = pltpu.VMEM((2, rows, nx, nz), jnp.float32)
    first, partial = pl.pallas_call(
        first_kernel,
        out_shape=(whole,) * 2,
        in_specs=[outside] * 7,
        out_specs=(outside,) * 2,
        scratch_shapes=[
            field, field, field, field,
            scalars[0], pltpu.SMEM(diffusivity.shape, jnp.float32), *scalars[1:],
            pltpu.VMEM((nx, ny, nz), jnp.float32),
            halo_y, halo_x, halo_y, halo_x, halo_y, pltpu.VMEM((4, rows, nz), jnp.float32), halo_x, halo_y,
            pltpu.SemaphoreType.DMA((9,)),
            pltpu.SemaphoreType.DMA((2,)),
            pltpu.SemaphoreType.DMA((12,)),
            pltpu.SemaphoreType.DMA((12,)),
        ],
        compiler_params=pltpu.CompilerParams(
            collective_id=0, has_side_effects=True, vmem_limit_bytes=60 * 1024 * 1024,
        ),
        name="sections",
    )(state, source_in, counts, diffusivity, log_rate, activation, heat_release)
    return pl.pallas_call(
        second_kernel,
        out_shape=(whole,) * 2,
        in_specs=[outside] * 6,
        out_specs=(outside,) * 2,
        scratch_shapes=[
            field, field, field, *scalars,
            pltpu.SemaphoreType.DMA((4,)),
            pltpu.SemaphoreType.DMA((nx // together,)),
            pltpu.SemaphoreType.DMA((2,)),
            pltpu.SemaphoreType.DMA((nx // together,)),
        ],
        compiler_params=pltpu.CompilerParams(vmem_limit_bytes=60 * 1024 * 1024),
        name="finish",
    )(first, partial, counts, log_rate, activation, heat_release)


def solution(mesh):
    grid = P(None, "gx", "gy", None)
    return jax.shard_map(
        local,
        mesh=mesh,
        in_specs=(grid, grid, P("gx", "gy"), P(), P(), P(), P()),
        out_specs=(grid, grid),
        check_vma=False,
    )
```

profile of v0, /device:TPU:0, one launch (start us, length us, event | category | flops | bytes accessed | tf_op | source)
XLA Modules:
  0.0 15.1 jit_solution(25117258935205172)
XLA Ops:
  0.6 12.0 %sections.1 = (f32[10,8,8,128]{3,2,1,0:T(8,128)}, f32[10,8,8,128]{3,2,1,0:T(8,128)}) custom-call(f32[10,8,8,128]{3,2,1,0:T(8,128)} %state.1, f32[10,8,8,128]{3,2,1,0:T(8,128)} %source.1, s32[8,8]{1,0:T(8,128)} %counts_in.3, f32[10]{0:T(128)} %diffusivity_in.1, f32[21]{0:T(128)} %log_rate_in.3, f32[21]{0:T(128)} %activation_in.3, f32[21]{0:T(128)} %heat_in.3), custom_call_target="tpu_custom_call" | custom-call | tf_op jit(solution)/shard_map/sections/pallas_call | solution.py:382
  12.7 2.4 %finish.1 = (f32[10,8,8,128]{3,2,1,0:T(8,128)}, f32[10,8,8,128]{3,2,1,0:T(8,128)}) custom-call(f32[10,8,8,128]{3,2,1,0:T(8,128)} %get-tuple-element.4.first_in, f32[10,8,8,128]{3,2,1,0:T(8,128)} %get-tuple-element.5.next_in, s32[8,8]{1,0:T(8,128)} %counts_in.3, f32[21]{0:T(128)} %log_rate_in.3, f32[21]{0:T(128)} %activation_in.3, f32[21]{0:T(128)} %heat_in.3), custom_call_target="tpu_custom_call" | custom-call | tf_op jit(solution)/shard_map/finish/pallas_call | solution.py:402
where the time goes:
time: 15.4 us; the launch traced here: 15.1 us
  Pallas kernels  14.4 us (94%)
  between operations  0.64 us (4%)
    pallas_call x1, Pallas kernels, local(): pl.pallas_call(first_kernel, out_shape=(whole,) * 2, in_specs=[outside] *...  12 us
    pallas_call x1, Pallas kernels, local(): pl.pallas_call(second_kernel, out_shape=(whole,) * 2, in_specs=[outside]...  2.41 us

commit v1 on v0

--- a/solution.py
+++ b/solution.py
@@ -147,11 +147,22 @@
     return number.astype(jnp.float32)
 
 
+def outer_laplace(halo_x, halo_y, k, i, at_low, at_high):
+    last = halo_y.shape[2] - 1
+    low = jnp.where(at_low, halo_y[0, k, pl.ds(i, 1), :], 0.0)
+    rest = jnp.where(at_high, halo_y[1, k, pl.ds(i, 1), :], low)
+    if i == 0:
+        rest = rest + halo_x[0, k]
+    if i == last:
+        rest = rest + halo_x[1, k]
+    return rest
+
+
 def first_kernel(
     state, source, counts_in, diffusivity_in, log_rate_in, activation_in, heat_in,
-    first_out, next_out,
+    first_out, next_out, hx2, hy2,
     st, src, first, nxt, counts, diffusivity, log_rate, activation, heat, numbers,
-    own_y, fx, fy, hx1, hy1, corners, hx2, hy2,
+    fx, fy, hx1, hy1, corners,
     load_sem, store_sem, send_sem, recv_sem,
 ):
     rows, nx, ny, nz = st.shape
@@ -167,7 +178,6 @@
     pairs = (
         (state, st), (source, src), (diffusivity_in, diffusivity),
         (counts_in, counts), (log_rate_in, log_rate), (activation_in, activation), (heat_in, heat),
-        (state.at[:, :, 0], own_y.at[0]), (state.at[:, :, ny - 1], own_y.at[1]),
     )
     loads = [pltpu.make_async_copy(one, two, load_sem.at[n]) for n, (one, two) in enumerate(pairs)]
     for load in loads:
@@ -213,15 +223,6 @@
             beside = beside + field[k, i + 1]
         return beside - 6.0 * here
 
-    def outer_laplace(halo_x, halo_y, k, i):
-        low = jnp.where(at_low, halo_y[0, k, pl.ds(i, 1), :], 0.0)
-        rest = jnp.where(at_high, halo_y[1, k, pl.ds(i, 1), :], low)
-        if i == 0:
-            rest = rest + halo_x[0, k]
-        if i == nx - 1:
-            rest = rest + halo_x[1, k]
-        return rest
-
     def first_inner(k, carry):
         weight = time_step * diffusivity[k]
         for i in range(nx):
@@ -261,57 +262,51 @@
     def first_outer(k, carry):
         weight = time_step * diffusivity[k]
         for i in range(nx):
-            first[k, i] = first[k, i] + weight * outer_laplace(hx1, hy1, k, i)
-        return carry
-
-    for copy in state_copies:
-        copy.wait()
+            first[k, i] = first[k, i] + weight * outer_laplace(hx1, hy1, k, i, at_low, at_high)
+        return carry
+
+    for copy in state_copies + corner_copies:
+        copy.wait_recv()
     lax.fori_loop(0, rows, first_outer, 0)
     first_store = pltpu.make_async_copy(first, first_out, store_sem.at[0])
     first_store.start()
 
     def next_inner(k, carry):
-        weight = (0.5 * time_step) * diffusivity[k]
-        for i in range(nx):
-            nxt[k, i] = (nxt[k, i] + 0.5 * first[k, i]) + weight * inner_laplace(first, k, i)
-        return carry
-
-    lax.fori_loop(0, rows, next_inner, 0)
-    for copy in corner_copies + first_copies:
-        copy.wait()
-
-    side_index = lax.broadcasted_iota(jnp.int32, (nx, nz), 0)
-
-    def next_outer(k, carry):
         weight = time_step * diffusivity[k]
         corner = [corners[n, pl.ds(k, 1), :] for n in range(4)]
-        for n, plane in ((0, st[k, 0]), (1, st[k, nx - 1])):
-            low = jnp.where(at_low, corner[2 * n], 0.0)
-            rest = jnp.where(at_high, corner[2 * n + 1], low)
-            hx2[n, k] = hx2[n, k] + weight * (plane + rest)
-        for n in range(2):
-            low = jnp.where(side_index == 0, corner[n], 0.0)
-            rest = jnp.where(side_index == nx - 1, corner[2 + n], low)
-            hy2[n, k] = hy2[n, k] + weight * (own_y[n, k] + rest)
         for i in range(nx):
-            nxt[k, i] = nxt[k, i] + (0.5 * weight) * outer_laplace(hx2, hy2, k, i)
-        return carry
-
-    lax.fori_loop(0, rows, next_outer, 0)
+            here = st[k, i]
+            edge = jnp.where(at_low | at_high, here, 0.0)
+            if i in (0, nx - 1):
+                n = 2 * (i // (nx - 1))
+                low = jnp.where(at_low, corner[n], 0.0)
+                edge = edge + here + 2.0 * jnp.where(at_high, corner[n + 1], low)
+            own = nxt[k, i] + 0.5 * first[k, i]
+            nxt[k, i] = own + (0.5 * weight) * (inner_laplace(first, k, i) + weight * edge)
+        return carry
+
+    lax.fori_loop(0, rows, next_inner, 0)
     next_store = pltpu.make_async_copy(nxt, next_out, store_sem.at[1])
     next_store.start()
+    for copy in first_copies:
+        copy.wait_recv()
+    for copy in state_copies + corner_copies + first_copies:
+        copy.wait_send()
     first_store.wait()
     next_store.wait()
 
 
 def second_kernel(
-    first_in, next_in, counts_in, log_rate_in, activation_in, heat_in,
+    first_in, next_in, hx_in, hy_in, counts_in, diffusivity_in, log_rate_in, activation_in, heat_in,
     next_out, late_out,
-    first, nxt, late, counts, log_rate, activation, heat, small_sem, load_sem, next_sem, late_sem,
+    first, nxt, late, hx, hy, counts, diffusivity, log_rate, activation, heat, small_sem, load_sem, next_sem, late_sem,
 ):
     rows, nx, ny, nz = first.shape
     groups = nx // together
-    pairs = ((counts_in, counts), (log_rate_in, log_rate), (activation_in, activation), (heat_in, heat))
+    pairs = (
+        (counts_in, counts), (diffusivity_in, diffusivity), (log_rate_in, log_rate), (activation_in, activation),
+        (heat_in, heat), (hx_in, hx), (hy_in, hy),
+    )
     small = [pltpu.make_async_copy(one, two, small_sem.at[n]) for n, (one, two) in enumerate(pairs)]
 
     def span(i):
@@ -327,12 +322,23 @@
     next_store = pltpu.make_async_copy(nxt, next_out, next_sem.at[1])
     for copy in small:
         copy.start()
+    next_load.start()
     for i in range(groups):
         first_load(i).start()
-    next_load.start()
+    row_index = lax.broadcasted_iota(jnp.int32, (ny, nz), 0)
+    at_low, at_high = row_index == 0, row_index == ny - 1
+
+    def next_outer(k, carry):
+        weight = (0.5 * time_step) * diffusivity[k]
+        for i in range(nx):
+            nxt[k, i] = nxt[k, i] + weight * outer_laplace(hx, hy, k, i, at_low, at_high)
+        return carry
+
     for copy in small:
         copy.wait()
-    row_index = lax.broadcasted_iota(jnp.int32, (ny, nz), 0)
+    next_load.wait()
+    lax.fori_loop(0, rows, next_outer, 0)
+    next_store.start()
 
     def group(i, carry):
         last = counts[i * together, 0]
@@ -357,12 +363,6 @@
             run(most_steps)
 
         late_store(i).start()
-
-        @pl.when(i == 0)
-        def _():
-            next_load.wait()
-            next_store.start()
-
         return carry
 
     lax.fori_loop(0, groups, group, 0)
@@ -379,17 +379,20 @@
     scalars = [pltpu.SMEM(a.shape, a.dtype) for a in (counts, log_rate, activation, heat_release)]
     halo_x = pltpu.VMEM((2, rows, ny, nz), jnp.float32)
     halo_y = pltpu.VMEM((2, rows, nx, nz), jnp.float32)
-    first, partial = pl.pallas_call(
+    wall_x = jax.ShapeDtypeStruct(halo_x.shape, jnp.float32)
+    wall_y = jax.ShapeDtypeStruct(halo_y.shape, jnp.float32)
+    spread = pltpu.SMEM(diffusivity.shape, jnp.float32)
+    first, partial, hx, hy = pl.pallas_call(
         first_kernel,
-        out_shape=(whole,) * 2,
+        out_shape=(whole, whole, wall_x, wall_y),
         in_specs=[outside] * 7,
-        out_specs=(outside,) * 2,
+        out_specs=(outside,) * 4,
         scratch_shapes=[
             field, field, field, field,
-            scalars[0], pltpu.SMEM(diffusivity.shape, jnp.float32), *scalars[1:],
+            scalars[0], spread, *scalars[1:],
             pltpu.VMEM((nx, ny, nz), jnp.float32),
-            halo_y, halo_x, halo_y, halo_x, halo_y, pltpu.VMEM((4, rows, nz), jnp.float32), halo_x, halo_y,
-            pltpu.SemaphoreType.DMA((9,)),
+            halo_x, halo_y, halo_x, halo_y, pltpu.VMEM((4, rows, nz), jnp.float32),
+            pltpu.SemaphoreType.DMA((7,)),
             pltpu.SemaphoreType.DMA((2,)),
             pltpu.SemaphoreType.DMA((12,)),
             pltpu.SemaphoreType.DMA((12,)),
@@ -402,18 +405,18 @@
     return pl.pallas_call(
         second_kernel,
         out_shape=(whole,) * 2,
-        in_specs=[outside] * 6,
+        in_specs=[outside] * 9,
         out_specs=(outside,) * 2,
         scratch_shapes=[
-            field, field, field, *scalars,
-            pltpu.SemaphoreType.DMA((4,)),
+            field, field, field, halo_x, halo_y, scalars[0], spread, *scalars[1:],
+            pltpu.SemaphoreType.DMA((7,)),
             pltpu.SemaphoreType.DMA((nx // together,)),
             pltpu.SemaphoreType.DMA((2,)),
             pltpu.SemaphoreType.DMA((nx // together,)),
         ],
         compiler_params=pltpu.CompilerParams(vmem_limit_bytes=60 * 1024 * 1024),
         name="finish",
-    )(first, partial, counts, log_rate, activation, heat_release)
+    )(first, partial, hx, hy, counts, diffusivity, log_rate, activation, heat_release)
 
 
 def solution(mesh):

time: 15.4 us -> 15.6 us (1.013)
  the two profiles are of different devices: /device:TPU:0 before, /device:TPU:1 now
where the time goes in v1:
time: 15.6 us; the launch traced here: 15.4 us
  Pallas kernels  14.8 us (95%)
  between operations  0.64 us (4%)
    pallas_call x1, Pallas kernels, local(): pl.pallas_call(first_kernel, out_shape=(whole, whole, wall_x, wall_y), in...  12 us
    pallas_call x1, Pallas kernels, local(): pl.pallas_call(second_kernel, out_shape=(whole,) * 2, in_specs=[outside]...  2.78 us

profile of v1, /device:TPU:1, one launch (start us, length us, event | category | flops | bytes accessed | tf_op | source)
XLA Modules:
  0.0 15.4 jit_solution(4787102114996349165)
XLA Ops:
  0.6 12.0 %sections.1 = (f32[10,8,8,128]{3,2,1,0:T(8,128)}, f32[10,8,8,128]{3,2,1,0:T(8,128)}, f32[2,10,8,128]{3,2,1,0:T(8,128)}, f32[2,10,8,128]{3,2,1,0:T(8,128)}) custom-call(f32[10,8,8,128]{3,2,1,0:T(8,128)} %state.1, f32[10,8,8,128]{3,2,1,0:T(8,128)} %source.1, s32[8,8]{1,0:T(8,128)} %counts_in.3, f32[10]{0:T(128)} %diffusivity_in.3, f32[21]{0:T(128)} %log_rate_in.3, ...), custom_call_target="tpu_custom_call" | custom-call | tf_op jit(solution)/shard_map/sections/pallas_call | solution.py:385
  12.6 2.8 %finish.1 = (f32[10,8,8,128]{3,2,1,0:T(8,128)}, f32[10,8,8,128]{3,2,1,0:T(8,128)}) custom-call(f32[10,8,8,128]{3,2,1,0:T(8,128)} %get-tuple-element.6.first_in, f32[10,8,8,128]{3,2,1,0:T(8,128)} %get-tuple-element.7.next_in, f32[2,10,8,128]{3,2,1,0:T(8,128)} %get-tuple-element.8.hx_in, f32[2,10,8,128]{3,2,1,0:T(8,128)} %get-tuple-element.9.hy_in, ...), custom_call_target="tpu_custom_call" | custom-call | tf_op jit(solution)/shard_map/finish/pallas_call | solution.py:405

commit v2 on v0

--- a/solution.py
+++ b/solution.py
@@ -151,7 +151,7 @@
     state, source, counts_in, diffusivity_in, log_rate_in, activation_in, heat_in,
     first_out, next_out,
     st, src, first, nxt, counts, diffusivity, log_rate, activation, heat, numbers,
-    own_y, fx, fy, hx1, hy1, corners, hx2, hy2,
+    own_x, own_y, own_corners, fx, fy, hx1, hy1, corners, hx2, hy2,
     load_sem, store_sem, send_sem, recv_sem,
 ):
     rows, nx, ny, nz = st.shape
@@ -167,7 +167,6 @@
     pairs = (
         (state, st), (source, src), (diffusivity_in, diffusivity),
         (counts_in, counts), (log_rate_in, log_rate), (activation_in, activation), (heat_in, heat),
-        (state.at[:, :, 0], own_y.at[0]), (state.at[:, :, ny - 1], own_y.at[1]),
     )
     loads = [pltpu.make_async_copy(one, two, load_sem.at[n]) for n, (one, two) in enumerate(pairs)]
     for load in loads:
@@ -185,19 +184,25 @@
             copy.start()
         return copies
 
+    def pack(k, carry):
+        for i in range(nx):
+            value = st[k, i]
+            own_y[0, k, pl.ds(i, 1), :] = value[ny - 1:]
+            own_y[1, k, pl.ds(i, 1), :] = value[:1]
+            if i in (0, nx - 1):
+                n = 0 if i == nx - 1 else 1
+                own_x[n, k] = value
+                own_corners[2 * n, k] = value[ny - 1:]
+                own_corners[2 * n + 1, k] = value[:1]
+        return carry
+
+    loads[0].wait()
+    lax.fori_loop(0, rows, pack, 0)
     pl.semaphore_wait(barrier, 8)
     state_copies = send((
-        (state.at[:, nx - 1], hx1.at[0]),
-        (state.at[:, 0], hx1.at[1]),
-        (state.at[:, :, ny - 1], hy1.at[0]),
-        (state.at[:, :, 0], hy1.at[1]),
+        (own_x.at[0], hx1.at[0]), (own_x.at[1], hx1.at[1]), (own_y.at[0], hy1.at[0]), (own_y.at[1], hy1.at[1]),
     ), sides, 0)
-    corner_copies = send((
-        (state.at[:, nx - 1, ny - 1], corners.at[0]),
-        (state.at[:, nx - 1, 0], corners.at[1]),
-        (state.at[:, 0, ny - 1], corners.at[2]),
-        (state.at[:, 0, 0], corners.at[3]),
-    ), diagonals, 4)
+    corner_copies = send(tuple((own_corners.at[n], corners.at[n]) for n in range(4)), diagonals, 4)
 
     row_index = lax.broadcasted_iota(jnp.int32, (ny, nz), 0)
     at_low, at_high = row_index == 0, row_index == ny - 1
@@ -235,7 +240,7 @@
                 fx[1, k] = value
         return carry
 
-    for load in loads[:3]:
+    for load in loads[1:3]:
         load.wait()
     lax.fori_loop(0, rows, first_inner, 0)
     first_copies = send((
@@ -265,7 +270,7 @@
         return carry
 
     for copy in state_copies:
-        copy.wait()
+        copy.wait_recv()
     lax.fori_loop(0, rows, first_outer, 0)
     first_store = pltpu.make_async_copy(first, first_out, store_sem.at[0])
     first_store.start()
@@ -278,13 +283,13 @@
 
     lax.fori_loop(0, rows, next_inner, 0)
     for copy in corner_copies + first_copies:
-        copy.wait()
+        copy.wait_recv()
 
     side_index = lax.broadcasted_iota(jnp.int32, (nx, nz), 0)
 
     def next_outer(k, carry):
         weight = time_step * diffusivity[k]
-        corner = [corners[n, pl.ds(k, 1), :] for n in range(4)]
+        corner = [corners[n, k] for n in range(4)]
         for n, plane in ((0, st[k, 0]), (1, st[k, nx - 1])):
             low = jnp.where(at_low, corner[2 * n], 0.0)
             rest = jnp.where(at_high, corner[2 * n + 1], low)
@@ -292,16 +297,22 @@
         for n in range(2):
             low = jnp.where(side_index == 0, corner[n], 0.0)
             rest = jnp.where(side_index == nx - 1, corner[2 + n], low)
-            hy2[n, k] = hy2[n, k] + weight * (own_y[n, k] + rest)
+            hy2[n, k] = hy2[n, k] + weight * (own_y[1 - n, k] + rest)
         for i in range(nx):
             nxt[k, i] = nxt[k, i] + (0.5 * weight) * outer_laplace(hx2, hy2, k, i)
         return carry
 
-    lax.fori_loop(0, rows, next_outer, 0)
-    next_store = pltpu.make_async_copy(nxt, next_out, store_sem.at[1])
-    next_store.start()
-    first_store.wait()
-    next_store.wait()
+    half = rows // 2
+    stores = [first_store]
+    for n in range(2):
+        lax.fori_loop(n * half, n * half + half, next_outer, 0)
+        part = pl.ds(n * half, half)
+        stores.append(pltpu.make_async_copy(nxt.at[part], next_out.at[part], store_sem.at[1 + n]))
+        stores[-1].start()
+    for copy in state_copies + corner_copies + first_copies:
+        copy.wait_send()
+    for store in stores:
+        store.wait()
 
 
 def second_kernel(
@@ -378,6 +389,7 @@
     outside = pl.BlockSpec(memory_space=pl.ANY)
     scalars = [pltpu.SMEM(a.shape, a.dtype) for a in (counts, log_rate, activation, heat_release)]
     halo_x = pltpu.VMEM((2, rows, ny, nz), jnp.float32)
+    corner = pltpu.VMEM((4, rows, 1, nz), jnp.float32)
     halo_y = pltpu.VMEM((2, rows, nx, nz), jnp.float32)
     first, partial = pl.pallas_call(
         first_kernel,
@@ -388,9 +400,9 @@
             field, field, field, field,
             scalars[0], pltpu.SMEM(diffusivity.shape, jnp.float32), *scalars[1:],
             pltpu.VMEM((nx, ny, nz), jnp.float32),
-            halo_y, halo_x, halo_y, halo_x, halo_y, pltpu.VMEM((4, rows, nz), jnp.float32), halo_x, halo_y,
-            pltpu.SemaphoreType.DMA((9,)),
-            pltpu.SemaphoreType.DMA((2,)),
+            halo_x, halo_y, corner, halo_x, halo_y, halo_x, halo_y, corner, halo_x, halo_y,
+            pltpu.SemaphoreType.DMA((7,)),
+            pltpu.SemaphoreType.DMA((3,)),
             pltpu.SemaphoreType.DMA((12,)),
             pltpu.SemaphoreType.DMA((12,)),
         ],

time: 15.4 us -> 15 us (0.974); the launches traced: 15.1 us -> 14.8 us
  Pallas kernels: 14.4 us -> 14.2 us
    pallas_call x1, Pallas kernels: 12 us -> 11.8 us  [local(): pl.pallas_call(first_kernel, out_shape=(whole,) * 2, in_specs=[outside] *...]
where the time goes in v2:
time: 15 us; the launch traced here: 14.8 us
  Pallas kernels  14.2 us (95%)
  between operations  0.64 us (4%)
    pallas_call x1, Pallas kernels, local(): pl.pallas_call(first_kernel, out_shape=(whole,) * 2, in_specs=[outside] *...  11.8 us
    pallas_call x1, Pallas kernels, local(): pl.pallas_call(second_kernel, out_shape=(whole,) * 2, in_specs=[outside]...  2.41 us

profile of v2, /device:TPU:0, one launch (start us, length us, event | category | flops | bytes accessed | tf_op | source)
XLA Modules:
  0.0 14.8 jit_solution(11613674154192460674)
XLA Ops:
  0.6 11.8 %sections.1 = (f32[10,8,8,128]{3,2,1,0:T(8,128)}, f32[10,8,8,128]{3,2,1,0:T(8,128)}) custom-call(f32[10,8,8,128]{3,2,1,0:T(8,128)} %state.1, f32[10,8,8,128]{3,2,1,0:T(8,128)} %source.1, s32[8,8]{1,0:T(8,128)} %counts_in.3, f32[10]{0:T(128)} %diffusivity_in.1, f32[21]{0:T(128)} %log_rate_in.3, f32[21]{0:T(128)} %activation_in.3, f32[21]{0:T(128)} %heat_in.3), custom_call_target="tpu_custom_call" | custom-call | tf_op jit(solution)/shard_map/sections/pallas_call | solution.py:394
  12.4 2.4 %finish.1 = (f32[10,8,8,128]{3,2,1,0:T(8,128)}, f32[10,8,8,128]{3,2,1,0:T(8,128)}) custom-call(f32[10,8,8,128]{3,2,1,0:T(8,128)} %get-tuple-element.4.first_in, f32[10,8,8,128]{3,2,1,0:T(8,128)} %get-tuple-element.5.next_in, s32[8,8]{1,0:T(8,128)} %counts_in.3, f32[21]{0:T(128)} %log_rate_in.3, f32[21]{0:T(128)} %activation_in.3, f32[21]{0:T(128)} %heat_in.3), custom_call_target="tpu_custom_call" | custom-call | tf_op jit(solution)/shard_map/finish/pallas_call | solution.py:414

commit v3 on v2

--- a/solution.py
+++ b/solution.py
@@ -334,13 +334,17 @@
     def late_store(i):
         return pltpu.make_async_copy(late.at[:, span(i)], late_out.at[:, span(i)], late_sem.at[i])
 
-    next_load = pltpu.make_async_copy(next_in, nxt, next_sem.at[0])
-    next_store = pltpu.make_async_copy(nxt, next_out, next_sem.at[1])
+    def next_load(i):
+        return pltpu.make_async_copy(next_in.at[:, span(i)], nxt.at[:, span(i)], next_sem.at[0, i])
+
+    def next_store(i):
+        return pltpu.make_async_copy(nxt.at[:, span(i)], next_out.at[:, span(i)], next_sem.at[1, i])
+
     for copy in small:
         copy.start()
     for i in range(groups):
         first_load(i).start()
-    next_load.start()
+        next_load(i).start()
     for copy in small:
         copy.wait()
     row_index = lax.broadcasted_iota(jnp.int32, (ny, nz), 0)
@@ -351,6 +355,8 @@
             for j in range(ny):
                 last = jnp.maximum(last, counts[i * together + n, j])
         number = jnp.stack([block_numbers(counts, i * together + n, row_index, ny) for n in range(together)])
+        next_load(i).wait()
+        next_store(i).start()
         first_load(i).wait()
 
         def run(upto):
@@ -368,17 +374,11 @@
             run(most_steps)
 
         late_store(i).start()
-
-        @pl.when(i == 0)
-        def _():
-            next_load.wait()
-            next_store.start()
-
         return carry
 
     lax.fori_loop(0, groups, group, 0)
-    next_store.wait()
     for i in range(groups):
+        next_store(i).wait()
         late_store(i).wait()
 
 
@@ -420,7 +420,7 @@
             field, field, field, *scalars,
             pltpu.SemaphoreType.DMA((4,)),
             pltpu.SemaphoreType.DMA((nx // together,)),
-            pltpu.SemaphoreType.DMA((2,)),
+            pltpu.SemaphoreType.DMA((2, nx // together)),
             pltpu.SemaphoreType.DMA((nx // together,)),
         ],
         compiler_params=pltpu.CompilerParams(vmem_limit_bytes=60 * 1024 * 1024),

time: 15 us -> 15 us (level)
  no operation moved by 1% of the time
where the time goes in v3:
time: 15 us; the launch traced here: 14.8 us
  Pallas kernels  14.2 us (95%)
  between operations  0.64 us (4%)
    pallas_call x1, Pallas kernels, local(): pl.pallas_call(first_kernel, out_shape=(whole,) * 2, in_specs=[outside] *...  11.8 us
    pallas_call x1, Pallas kernels, local(): pl.pallas_call(second_kernel, out_shape=(whole,) * 2, in_specs=[outside]...  2.41 us

profile of v3, /device:TPU:0, one launch (start us, length us, event | category | flops | bytes accessed | tf_op | source)
XLA Modules:
  0.0 14.8 jit_solution(13629801838298215326)
XLA Ops:
  0.6 11.8 %sections.1 = (f32[10,8,8,128]{3,2,1,0:T(8,128)}, f32[10,8,8,128]{3,2,1,0:T(8,128)}) custom-call(f32[10,8,8,128]{3,2,1,0:T(8,128)} %state.1, f32[10,8,8,128]{3,2,1,0:T(8,128)} %source.1, s32[8,8]{1,0:T(8,128)} %counts_in.3, f32[10]{0:T(128)} %diffusivity_in.1, f32[21]{0:T(128)} %log_rate_in.3, f32[21]{0:T(128)} %activation_in.3, f32[21]{0:T(128)} %heat_in.3), custom_call_target="tpu_custom_call" | custom-call | tf_op jit(solution)/shard_map/sections/pallas_call | solution.py:394
  12.4 2.4 %finish.1 = (f32[10,8,8,128]{3,2,1,0:T(8,128)}, f32[10,8,8,128]{3,2,1,0:T(8,128)}) custom-call(f32[10,8,8,128]{3,2,1,0:T(8,128)} %get-tuple-element.4.first_in, f32[10,8,8,128]{3,2,1,0:T(8,128)} %get-tuple-element.5.next_in, s32[8,8]{1,0:T(8,128)} %counts_in.3, f32[21]{0:T(128)} %log_rate_in.3, f32[21]{0:T(128)} %activation_in.3, f32[21]{0:T(128)} %heat_in.3), custom_call_target="tpu_custom_call" | custom-call | tf_op jit(solution)/shard_map/finish/pallas_call | solution.py:414
